TPU v7x, 32 devices: a whole 2x2x4 slice. The times are simulated.
32 devices in a mesh: rows: 16 (over z, y, x), batch: 2 (over core).
Axes of the slice: x: 2, y: 2, z: 4, core: 2. Of those that a mesh axis runs over, the one named last changes fastest.
Arguments:
- frames: bfloat16 [4096, 1024], P('rows', 'batch'), may hold values from -40 to 40
- tap_table: int32 [63], replicated, may hold values from -128 to 127
- sketch_matrix: bfloat16 [512, 256], replicated, may hold values from -0.25 to 0.25
- decay_rates: float32 [2, 256], P('batch'), may hold values from 0.5 to 1
Outputs:
- basis: float32 [2, 4096, 256], P('batch', 'rows')
- factor: float32 [2, 256, 256], P('batch')
- coeffs: float32 [2, 256, 512], P('batch')
All inputs are finite; a program needn't handle non-finite values.
Results may differ from a plain program's by a relative error of at most 0.0039.
The roundings to bfloat16 on the way count: a program that leaves them out, or rounds other values in their place, can miss the bound.
Values may be sent and summed in bfloat16 or wider, within the bound.
A program may use at most 64 MiB of HBM per device.

v0:
```python
import math

import jax
import jax.numpy as jnp
from jax import lax
from jax.sharding import PartitionSpec as P

HIGH = lax.Precision.HIGHEST


def passed_along(x, axis, by):
    length = lax.axis_size(axis)
    pairs = [(i, i + by) for i in range(length) if 0 <= i + by < length]
    return lax.ppermute(x, axis, pairs)


def band_matrix(coefs, rows_count, cols_count, offset):
    row_ids = lax.broadcasted_iota(jnp.int32, (rows_count, cols_count), 0)
    col_ids = lax.broadcasted_iota(jnp.int32, (rows_count, cols_count), 1)
    lag_ids = col_ids - row_ids + offset
    valid = (lag_ids >= 0) & (lag_ids < coefs.shape[0])
    values = jnp.take(coefs, jnp.clip(lag_ids, 0, coefs.shape[0] - 1))
    return jnp.where(valid, values, jnp.zeros_like(values))


def gram_of(block):
    return lax.dot_general(
        block, block, (((0,), (0,)), ((), ())), precision=HIGH, preferred_element_type=jnp.float32
    )


def cross_of(left, right):
    return lax.dot_general(
        left, right, (((0,), (0,)), ((), ())), precision=HIGH, preferred_element_type=jnp.float32
    )


def shards(frames, tap_table, sketch_matrix, decay_rates):
    rows_here, frame_count = frames.shape
    tap_count = tap_table.shape[0]
    npoints = rows_here * lax.axis_size("rows")
    batch_count = lax.axis_size("batch")
    coefs = (tap_table.astype(jnp.float32) / 1024.0).astype(jnp.bfloat16)
    main_band = band_matrix(coefs, frame_count, frame_count, 0)
    hist_band = band_matrix(coefs, tap_count - 1, frame_count, tap_count - 1)
    history = passed_along(frames[:, frame_count - (tap_count - 1) :], "batch", 1)
    filtered = (
        jnp.dot(frames, main_band, preferred_element_type=jnp.float32)
        + jnp.dot(history, hist_band, preferred_element_type=jnp.float32)
    ).astype(jnp.bfloat16)
    sketched = jnp.dot(filtered, sketch_matrix, preferred_element_type=jnp.float32)
    rates = decay_rates[0]

    def one_turn(turn_index, carried):
        return rates[None, :] * passed_along(carried, "batch", 1) + sketched

    weighted = lax.fori_loop(0, batch_count - 1, one_turn, sketched)
    root_points = math.sqrt(npoints)
    rank_count = weighted.shape[1]
    filtered_wide = filtered.astype(jnp.float32)
    gram_total, cross_total = lax.psum(
        (gram_of(weighted), cross_of(weighted, filtered_wide)), "rows"
    )
    lower_one = jnp.linalg.cholesky(gram_total)
    final_q = lax.linalg.triangular_solve(
        lower_one, weighted, left_side=False, lower=True, transpose_a=True
    )
    scaled = final_q * root_points
    step_one = lax.linalg.triangular_solve(lower_one, cross_total, left_side=True, lower=True)
    projected = step_one * (math.sqrt(rank_count) / root_points)
    upper = lower_one.T / root_points
    return (scaled[None], upper[None], projected[None])


def solution(mesh):
    placed = (P("rows", "batch"), P(), P(), P("batch", None))
    return jax.shard_map(
        shards,
        mesh=mesh,
        in_specs=placed,
        out_specs=(P("batch", "rows", None), P("batch", None, None), P("batch", None, None)),
        check_vma=False,
    )
```

profile of v0, /device:TPU:0, one launch (start us, length us, event | category | flops | bytes accessed | tf_op | source)
XLA Modules:
  0.0 432.6 jit_solution(13166161007470643406)
XLA Ops:
  7.2 0.9 slice.55
  8.2 2.4 collective-permute-start
  10.6 0.7 fusion.425
  11.3 0.7 fusion.426
  12.0 0.7 fusion.423
  12.7 0.7 fusion.424
  13.5 0.9 copy-done.3
  14.4 41.2 %fusion.190 = f32[512,256]{1,0:T(8,128)S(1)} fusion(bf16[256,512]{1,0:T(8,128)(2,1)S(1)} %copy-done.3, bf16[]{:T(256)} %bitcast.113, bf16[]{:T(256)} %bitcast.114, bf16[]{:T(256)} %bitcast.115, bf16[]{:T(256)} %bitcast.116, bf16[]{:T(256)} %bitcast.117, bf16[]{:T(256)} %bitcast.119, bf16[]{:T(256)} %bitcast.118, bf16[]{:T(256)} %bitcast.2, bf16[]{:T(256)} %bitcast.4, ...), kind=kOutput, calls=%fused_computation.200 | convolution fusion | flops 171442176 | bytes 786558 | tf_op jit(solution)/shard_map/dot_general | solution.py:48
  55.7 185.6 %gather_fusion = bf16[31744]{0:T(1024)(128)(2,1)S(1)} fusion(bf16[63]{0:T(256)(128)(2,1)S(1)} %multiply_convert_fusion, s32[31744]{0:T(1024)S(1)} %broadcast_clamp_fusion), kind=kCustom, calls=%fused_computation | custom fusion | bytes 253952 | tf_op jit(solution)/shard_map/jit(_take)/gather | solution.py:22
  241.9 1.5 collective-permute-start.1
  243.4 0.9 collective-permute-done.1
  244.4 1.3 fusion.428
  245.7 1.4 fusion.429
  247.2 112.8 %all-reduce.4.cloned.1.call-done = (f32[256,256]{0,1:T(8,128)}, f32[256,512]{1,0:T(8,128)}) async-done(((f32[256,256]{0,1:T(8,128)}, f32[256,512]{1,0:T(8,128)}), (f32[256,256]{0,1:T(8,128)}, f32[256,512]{1,0:T(8,128)})) %all-reduce.4.cloned.1.call-update) | async-done | bytes 786448 | tf_op jit(solution)/shard_map/psum | solution.py:61
  360.0 1.1 copy.12
  361.2 11.7 %cholesky.50 = f32[128,128]{1,0:T(8,128)S(1)} custom-call(f32[128,128]{1,0:T(8,128)S(1)} %cholesky.118), custom_call_target="Cholesky" | custom-call | tf_op jit(solution)/shard_map/jit(cholesky)/cholesky | solution.py:64
  373.0 9.8 %custom-call.16 = f32[1,128,128]{1,2,0:T(8,128)S(1)} custom-call(f32[1,128,128]{2,1,0:T(8,128)S(1)} %get-tuple-element.46), custom_call_target="InvertDiagBlocksLowerTriangular" | custom-call | tf_op jit(solution)/shard_map/jit(cholesky)/cholesky | solution.py:64
  383.3 11.7 %cholesky.105 = f32[128,128]{1,0:T(8,128)S(1)} custom-call(f32[128,128]{1,0:T(8,128)S(1)} %convolution_subtract_fusion), custom_call_target="Cholesky" | custom-call | tf_op jit(solution)/shard_map/jit(cholesky)/cholesky | solution.py:64
  395.0 0.6 compare_reduce_fusion
  397.1 4.2 while.1
  397.3 0.6 fusion.443
  397.9 1.4 bitcast_dynamic-update-slice_fusion.2
  399.3 0.6 fusion.443
  399.9 1.4 bitcast_dynamic-update-slice_fusion.2
  401.3 19.7 %custom-call.17 = f32[2,128,128]{1,2,0:T(8,128)S(1)} custom-call(f32[2,128,128]{2,1,0:T(8,128)S(1)} %get-tuple-element.22), custom_call_target="InvertDiagBlocksLowerTriangular" | custom-call | tf_op jit(solution)/shard_map/triangular_solve | solution.py:65
  421.3 0.4 fusion.347
  422.0 0.8 copy.13
  422.9 0.8 copy.14
  423.7 0.4 fusion.259
  424.1 0.4 fusion.345
  424.5 0.4 convolution_bitcast_fusion
  424.9 0.8 maximum_multiply_fusion
  (38 shorter events, 2.1 us)
Async XLA Ops:
  7.2 234.5 %copy-start = (bf16[512,256]{1,0:T(8,128)(2,1)S(1)}, bf16[512,256]{1,0:T(8,128)(2,1)}, u32[]{:S(2)}) copy-start(bf16[512,256]{1,0:T(8,128)(2,1)} %param.6) | copy-start | bytes 786436
  7.2 3.4 copy-start.5
  7.2 352.8 %all-reduce.4.cloned.1.call-start = ((), (), s32[]{:S(2)}) async-start(), calls=%async_computation | async-start | bytes 1572864 | tf_op jit(solution)/shard_map/psum | solution.py:61
  8.2 233.2 %collective-permute-start = (bf16[256,62]{1,0:T(8,128)(2,1)S(1)}, bf16[256,62]{1,0:T(8,128)(2,1)S(1)}, u32[]{:S(2)}, u32[]{:S(2)}) collective-permute-start(bf16[256,62]{1,0:T(8,128)(2,1)S(1)} %slice.55), channel_id=1, source_target_pairs={{0,1},{2,3},{4,5},{6,7},{8,9},{10,11},{12,13},{14,15},{16,17},{18,... | collective-permute-start | bytes 95240 | tf_op jit(solution)/shard_map/ppermute | solution.py:14
  13.4 1.0 copy-start.3
  241.9 2.5 copy-start.4
  241.9 2.4 collective-permute-start.1
  360.0 1.2 copy-start.1
  422.0 1.7 copy-start.2
Sparse Core Ops, SparseCore 0:
  247.3 112.6 all-reduce.3
where the time goes:
time: 433 us
  local copies, waits for them, and re-layouts  197 us (45%)
  waiting for transfers between devices  114 us (26%)
  other arithmetic  54.6 us (13%)
  matrix products  47.2 us (11%)
  between operations  15.6 us (4%)
    gather x6, local copies, waits for them, and re-layouts, band_matrix(): values = jnp.take(coefs, jnp.clip(lag_ids, 0, coefs.shape[0] - 1))  189 us
    psum x1, waiting for transfers between devices, shards(): lax.psum((gram_of(weighted), cross_of(weighted, filtered_wide)), 'rows')  113 us
    dot_general x1, matrix products, shards(): jnp.dot(frames, main_band, preferred_element_type=jnp.float32)  41.2 us
    another operation x6, other arithmetic, shards(): lower_one = jnp.linalg.cholesky(gram_total)  33.9 us
    another operation x2, other arithmetic, shards(): lax.linalg.triangular_solve(lower_one, weighted, left_side=False, lower=T...  19.7 us
  transfers between devices with their start and end apart: 3, of which 2 were waited for; matrix products, arithmetic and copies ran while one was open for 53% of the time, Pallas kernels for 0%

commit v1 on v0

v1 whole, which is shorter than its diff:
```python
import functools
import math

import jax
import jax.numpy as jnp
from jax import lax
from jax.experimental import pallas as pl
from jax.experimental.pallas import tpu as pltpu
from jax.sharding import PartitionSpec as P

MESH = pl.DeviceIdType.MESH
HIGHEST = lax.Precision.HIGHEST
F32 = jnp.float32
BF16 = jnp.bfloat16
LANES = 128
PANEL = 8
VMEM_SPEC = pl.BlockSpec(memory_space=pltpu.VMEM)


def greet(count, batches, with_batch):
    row, turn = lax.axis_index("rows"), lax.axis_index("batch")
    barrier = pltpu.get_barrier_semaphore()
    for step in range(1, count):
        pl.semaphore_signal(
            barrier, inc=1, device_id=(lax.rem(row + step, count), turn), device_id_type=MESH
        )
    waits = count - 1
    if with_batch and batches > 1:

        @pl.when(turn > 0)
        def _():
            pl.semaphore_signal(barrier, inc=1, device_id=(row, turn - 1), device_id_type=MESH)

        @pl.when(turn < batches - 1)
        def _():
            pl.semaphore_signal(barrier, inc=1, device_id=(row, turn + 1), device_id_type=MESH)

        waits = waits + jnp.where(turn > 0, 1, 0) + jnp.where(turn < batches - 1, 1, 0)
    pl.semaphore_wait(barrier, waits)


def exchange(count, source_of, target_of, send_sems, recv_sems):
    row, turn = lax.axis_index("rows"), lax.axis_index("batch")
    copies = []
    for step in range(1, count):
        peer = lax.rem(row + step, count)
        copy = pltpu.make_async_remote_copy(
            src_ref=source_of(peer),
            dst_ref=target_of(row),
            send_sem=send_sems.at[step],
            recv_sem=recv_sems.at[step],
            device_id=(peer, turn),
            device_id_type=MESH,
        )
        copy.start()
        copies.append(copy)
    return copies


def sum_over_rows(count, parts, landed, total, send_a, recv_a, send_b, recv_b):
    row = lax.axis_index("rows")
    first = exchange(
        count, lambda peer: parts.at[peer], lambda mine: landed.at[mine], send_a, recv_a
    )
    landed[row] = parts[row]
    for copy in first:
        copy.wait_recv()
    summed = landed[0].astype(F32)
    for sender in range(1, count):
        summed = summed + landed[sender].astype(F32)
    total[row] = summed.astype(total.dtype)
    second = exchange(
        count, lambda peer: total.at[row], lambda mine: total.at[mine], send_b, recv_b
    )
    for copy in second:
        copy.wait_recv()
    for copy in first + second:
        copy.wait_send()


def sketch_kernel(
    count, batches, shard,
    frames, taps, sketch, rates, gram_out, weighted, filtered,
    tap_row, history, before, parts, landed, total, hist_sems, prev_sems, send_a, recv_a, send_b, recv_b,
):
    row, turn = lax.axis_index("rows"), lax.axis_index("batch")
    frame_count = frames.shape[1]
    rank = sketch.shape[1]
    greet(count, batches, True)

    def hist_copy():
        return pltpu.make_async_remote_copy(
            src_ref=frames.at[:, pl.ds(frame_count - LANES, LANES)],
            dst_ref=history,
            send_sem=hist_sems.at[0],
            recv_sem=hist_sems.at[1],
            device_id=(row, turn + 1),
            device_id_type=MESH,
        )

    def prev_copy():
        return pltpu.make_async_remote_copy(
            src_ref=weighted,
            dst_ref=before,
            send_sem=prev_sems.at[0],
            recv_sem=prev_sems.at[1],
            device_id=(row, turn + 1),
            device_id_type=MESH,
        )

    @pl.when(turn < batches - 1)
    def _():
        hist_copy().start()

    tap_row[...] = jnp.zeros_like(tap_row)
    tap_row[:, : taps.shape[1]] = taps[...].astype(F32) / 1024.0
    spread = jnp.broadcast_to(tap_row[...], (LANES, tap_row.shape[1]))
    rolled = pltpu.roll(spread, 0, 1, stride=1, stride_axis=0)
    wide = tap_row.shape[1]
    after = jnp.concatenate([rolled[:, wide - LANES :], rolled[:, :LANES]], axis=1)
    band = jnp.concatenate([rolled[:, LANES : 3 * LANES], rolled[:, : 2 * LANES], after], axis=0).astype(BF16)

    step = 2 * LANES
    for start in range(step, frame_count, step):
        filtered[:, start : start + step] = jnp.dot(
            frames[:, start - LANES : start + step], band, preferred_element_type=F32
        ).astype(BF16)
    here = jnp.dot(frames[:, :step], band[LANES:], preferred_element_type=F32)

    @pl.when(turn == 0)
    def _():
        history[...] = jnp.zeros_like(history)

    @pl.when(turn > 0)
    def _():
        hist_copy().wait_recv()

    filtered[:, :step] = (
        here + jnp.dot(history[...], band[:LANES], preferred_element_type=F32)
    ).astype(BF16)
    sketched = jnp.dot(filtered[...], sketch[...], preferred_element_type=F32)
    weighted[...] = sketched

    @pl.when(turn > 0)
    def _():
        prev_copy().wait_recv()
        weighted[...] = rates[...] * before[...] + weighted[...]

    @pl.when(turn < batches - 1)
    def _():
        prev_copy().start()

    value = weighted[...]
    gram = jnp.dot(value.T, value, precision=HIGHEST, preferred_element_type=F32)
    half = rank // 2
    blocks = [gram[:half, :half], gram[:half, half:], gram[half:, half:]]
    packed = jnp.concatenate(blocks, axis=0)
    for index in range(count):
        low = index * shard
        if low < packed.shape[0]:
            parts[index] = packed[low : low + shard]
        else:
            parts[index] = jnp.zeros((shard, half), F32)
    sum_over_rows(count, parts, landed, total, send_a, recv_a, send_b, recv_b)
    for index in range(count):
        low = index * shard
        if low < packed.shape[0]:
            gram_out[low : low + shard] = total[index]

    @pl.when(turn < batches - 1)
    def _():
        hist_copy().wait_send()
        prev_copy().wait_send()


def pieces(x):
    high = x.astype(BF16).astype(F32)
    rest = x - high
    mid = rest.astype(BF16).astype(F32)
    return high, mid, rest - mid


def eliminate(work, upper, inverse, begin, wide):
    rank = work.shape[0]
    first = begin
    last = rank + begin + LANES

    def panel(index, _):
        offset = pl.multiple_of(index * PANEL, PANEL)
        rows = pl.ds(pl.multiple_of(begin + offset, PANEL), PANEL)
        block = work[rows, first:last]
        corner = pltpu.roll(block[:, :LANES], lax.rem(LANES - offset, LANES), 1)
        full = (PANEL, LANES)
        columns = [jnp.broadcast_to(corner[:, j : j + 1], full) for j in range(PANEL)]
        held = {
            (i, j): jnp.broadcast_to(columns[j][i : i + 1], full)
            for j in range(PANEL)
            for i in range(j, PANEL)
        }
        lines = [jnp.broadcast_to(block[i : i + 1], block.shape) for i in range(PANEL)]
        copies = block.shape[1] // LANES
        place = lax.broadcasted_iota(jnp.int32, block.shape, 0)
        result = jnp.zeros_like(block)
        for j in range(PANEL):
            scale = lax.rsqrt(held[j, j])
            factors = {i: held[i, j] * scale for i in range(j + 1, PANEL)}
            for i in range(j + 1, PANEL):
                for k in range(j + 1, i + 1):
                    held[i, k] = held[i, k] - factors[i] * factors[k]
            done = lines[j] * jnp.concatenate([scale] * copies, axis=1)
            for i in range(j + 1, PANEL):
                lines[i] = lines[i] - jnp.concatenate([factors[i]] * copies, axis=1) * done
            result = jnp.where(place == j, done, result)
        upper[rows, first:rank] = result[:, : rank - first]
        inverse[rows, : begin + LANES] = result[:, rank - first :]
        high, mid, low = pieces(result)
        width = rank - first
        left = jnp.concatenate([high, high, mid, high, mid, low], axis=0)[:, :width].astype(BF16)
        right = jnp.concatenate([high, mid, high, low, mid, high], axis=0).astype(BF16)
        work[first:, first:last] = work[first:, first:last] - lax.dot_general(
            left, right, (((0,), (0,)), ((), ())), preferred_element_type=F32
        )
        return 0

    lax.fori_loop(0, LANES // PANEL, panel, 0)


def factor_kernel(npoints, gram, weighted, filtered, basis, factor, partial, work, upper, inverse):
    rank = weighted.shape[1]
    half = rank // 2
    across = gram[half:rank, :]
    work[:half, :half] = gram[:half, :]
    work[:half, half:rank] = across
    work[half:, :half] = across.T
    work[half:, half:rank] = gram[rank:, :]
    ids = lax.broadcasted_iota(jnp.int32, (rank, rank), 0)
    cols = lax.broadcasted_iota(jnp.int32, (rank, rank), 1)
    work[:, rank:] = jnp.where(ids == cols, 1.0, 0.0).astype(F32)
    upper[...] = jnp.zeros_like(upper)
    inverse[...] = jnp.zeros_like(inverse)
    for begin in range(0, rank, LANES):
        eliminate(work, upper, inverse, begin, LANES)
    root = math.sqrt(npoints)
    factor[0] = jnp.where(cols >= ids, upper[...], 0.0) * (1.0 / root)
    scaled = lax.dot_general(
        weighted[...], inverse[...], (((1,), (1,)), ((), ())), precision=HIGHEST, preferred_element_type=F32
    ) * root
    basis[0] = scaled
    high = scaled.astype(BF16)
    low = (scaled - high.astype(F32)).astype(BF16)
    turned = filtered[...].T
    cross = jnp.dot(turned, high, preferred_element_type=F32) + jnp.dot(turned, low, preferred_element_type=F32)
    partial[...] = (cross * (math.sqrt(rank) / npoints)).astype(partial.dtype)


def coeffs_kernel(count, batches, shard, partial, out, parts, landed, total, send_a, recv_a, send_b, recv_b):
    greet(count, batches, False)
    for index in range(count):
        low = index * shard
        if low < partial.shape[0]:
            parts[index] = partial[low : low + shard]
        else:
            parts[index] = jnp.zeros((shard, partial.shape[1]), partial.dtype)
    sum_over_rows(count, parts, landed, total, send_a, recv_a, send_b, recv_b)
    for index in range(count):
        low = index * shard
        if low < partial.shape[0]:
            out[low : low + shard] = total[index]


def shard_rows(length, count, tile):
    return tile * -(-length // (tile * count))


def sems(count):
    return [pltpu.SemaphoreType.DMA((count,)) for _ in range(4)]


def shards(frames, tap_table, sketch_matrix, decay_rates):
    count, batches = lax.axis_size("rows"), lax.axis_size("batch")
    rows_here, frame_count = frames.shape
    rank = sketch_matrix.shape[1]
    half = rank // 2
    npoints = rows_here * count
    shard = shard_rows(3 * half, count, 8)
    slots = (count, shard, half)
    limit = 48 * 1024 * 1024
    gram, weighted, filtered = pl.pallas_call(
        functools.partial(sketch_kernel, count, batches, shard),
        out_shape=(
            jax.ShapeDtypeStruct((3 * half, half), F32),
            jax.ShapeDtypeStruct((rows_here, rank), F32),
            jax.ShapeDtypeStruct((rows_here, frame_count), BF16),
        ),
        in_specs=[VMEM_SPEC] * 4,
        out_specs=(VMEM_SPEC,) * 3,
        scratch_shapes=[
            pltpu.VMEM((1, 4 * LANES), F32),
            pltpu.VMEM((rows_here, LANES), BF16),
            pltpu.VMEM((rows_here, rank), F32),
            pltpu.VMEM(slots, F32),
            pltpu.VMEM(slots, F32),
            pltpu.VMEM(slots, F32),
            pltpu.SemaphoreType.DMA((2,)),
            pltpu.SemaphoreType.DMA((2,)),
        ] + sems(count),
        compiler_params=pltpu.CompilerParams(
            collective_id=0, has_side_effects=True, vmem_limit_bytes=limit
        ),
        name="sketch",
    )(frames, tap_table.reshape(1, -1), sketch_matrix, decay_rates)
    basis, factor, partial = pl.pallas_call(
        functools.partial(factor_kernel, npoints),
        out_shape=(
            jax.ShapeDtypeStruct((1, rows_here, rank), F32),
            jax.ShapeDtypeStruct((1, rank, rank), F32),
            jax.ShapeDtypeStruct((frame_count, rank), BF16),
        ),
        in_specs=[VMEM_SPEC] * 3,
        out_specs=(VMEM_SPEC,) * 3,
        scratch_shapes=[
            pltpu.VMEM((rank, 2 * rank), F32),
            pltpu.VMEM((rank, rank), F32),
            pltpu.VMEM((rank, rank), F32),
        ],
        compiler_params=pltpu.CompilerParams(vmem_limit_bytes=limit),
        name="factor",
    )(gram, weighted, filtered)
    shard = shard_rows(frame_count, count, 16)
    slots = (count, shard, rank)
    turned = pl.pallas_call(
        functools.partial(coeffs_kernel, count, batches, shard),
        out_shape=jax.ShapeDtypeStruct((frame_count, rank), BF16),
        in_specs=[VMEM_SPEC],
        out_specs=VMEM_SPEC,
        scratch_shapes=[pltpu.VMEM(slots, BF16)] * 3 + sems(count),
        compiler_params=pltpu.CompilerParams(
            collective_id=1, has_side_effects=True, vmem_limit_bytes=limit
        ),
        name="coeffs",
    )(partial)
    return (basis, factor, turned.T.astype(F32)[None])


def solution(mesh):
    placed = (P("rows", "batch"), P(), P(), P("batch", None))
    return jax.shard_map(
        shards,
        mesh=mesh,
        in_specs=placed,
        out_specs=(P("batch", "rows", None), P("batch", None, None), P("batch", None, None)),
        check_vma=False,
    )
```

time: 433 us -> 59.6 us (0.14)
  local copies, waits for them, and re-layouts: 197 us -> 3.56 us
  waiting for transfers between devices: 114 us -> 0 us
  Pallas kernels: 0 us -> 55.2 us
  other arithmetic: 54.6 us -> 0.04 us
  matrix products: 47.2 us -> 0 us
  between operations: 15.6 us -> 0.67 us
    gather x6 -> x0, local copies, waits for them, and re-layouts: 189 us -> none  [band_matrix(): values = jnp.take(coefs, jnp.clip(lag_ids, 0, coefs.shape[0] - 1))]
    psum x1 -> x0, waiting for transfers between devices: 113 us -> none  [shards(): lax.psum((gram_of(weighted), cross_of(weighted, filtered_wide)), 'rows')]
    pallas_call x0 -> x3, Pallas kernels: none -> 55.2 us  [the longest x1 20.3 us: shards(): pl.pallas_call(functools.partial(sketch_kernel, count, batches, shard), o...]
    another operation x8 -> x0, other arithmetic: 53.6 us -> none  [the longest x6 33.9 us: shards(): lower_one = jnp.linalg.cholesky(gram_total)]
    dot_general x5 -> x0, matrix products: 44.5 us -> none  [the longest x1 41.2 us: shards(): jnp.dot(frames, main_band, preferred_element_type=jnp.float32)]
  transfers between devices with their start and end apart: 3 -> 0, of which waited for: 2 -> 0; matrix products, arithmetic and copies ran while one was open for 53% -> 0% of each run, Pallas kernels for 0% -> 0%
where the time goes in v1:
time: 59.6 us; the launch traced here: 59.4 us
  Pallas kernels  55.2 us (93%)
  local copies, waits for them, and re-layouts  3.56 us (6%)
  between operations  0.67 us (1%)
    pallas_call x1, Pallas kernels, shards(): pl.pallas_call(functools.partial(sketch_kernel, count, batches, shard), o...  20.3 us
    pallas_call x1, Pallas kernels, shards(): pl.pallas_call(functools.partial(coeffs_kernel, count, batches, shard), o...  18.1 us
    pallas_call x1, Pallas kernels, shards(): pl.pallas_call(functools.partial(factor_kernel, npoints), out_shape=(jax....  16.8 us
    unnamed x9, local copies, waits for them, and re-layouts  3.56 us

profile of v1, /device:TPU:0, one launch (start us, length us, event | category | flops | bytes accessed | tf_op | source)
XLA Modules:
  0.0 59.4 jit_solution(1498643451152871906)
XLA Ops:
  0.6 0.0 copy-start.2
  0.6 0.0 copy-start.3
  0.7 0.7 %copy-done.2 = f32[1,256]{1,0:T(1,128)S(1)} copy-done((f32[1,256]{1,0:T(1,128)S(1)}, f32[1,256]{1,0:T(1,128)}, u32[]{:S(2)}) %copy-start.2) | copy-done | bytes 1048
  1.3 0.0 copy-done.3
  1.3 0.0 copy-start
  1.3 0.9 %copy-done = bf16[256,512]{1,0:T(8,128)(2,1)S(1)} copy-done((bf16[256,512]{1,0:T(8,128)(2,1)S(1)}, bf16[256,512]{1,0:T(8,128)(2,1)}, u32[]{:S(2)}) %copy-start) | copy-done | bytes 262168
  2.3 0.0 copy-start.1
  2.3 0.9 %copy-done.1 = bf16[512,256]{1,0:T(8,128)(2,1)S(1)} copy-done((bf16[512,256]{1,0:T(8,128)(2,1)S(1)}, bf16[512,256]{1,0:T(8,128)(2,1)}, u32[]{:S(2)}) %copy-start.1) | copy-done | bytes 262168
  3.2 20.3 %sketch.2 = (f32[384,128]{1,0:T(8,128)S(1)}, f32[256,256]{1,0:T(8,128)S(1)}, bf16[256,512]{1,0:T(8,128)(2,1)S(1)}) custom-call(bf16[256,512]{1,0:T(8,128)(2,1)S(1)} %copy-done, s32[1,63]{1,0:T(1,128)S(1)} %bitcast.5, bf16[512,256]{1,0:T(8,128)(2,1)S(1)} %copy-done.1, f32[1,256]{1,0:T(1,128)S(1)} %copy-done.2), custom_call_target="tpu_custom_call" | custom-call | tf_op jit(solution)/shard_map/sketch/pallas_call | solution.py:288
  23.5 16.8 %factor.1 = (f32[1,256,256]{2,1,0:T(8,128)}, f32[1,256,256]{2,1,0:T(8,128)}, bf16[512,256]{1,0:T(8,128)(2,1)S(1)}) custom-call(f32[384,128]{1,0:T(8,128)S(1)} %get-tuple-element.9.gram, f32[256,256]{1,0:T(8,128)S(1)} %get-tuple-element.10.weighted, bf16[256,512]{1,0:T(8,128)(2,1)S(1)} %get-tuple-element.11.filtered), custom_call_target="tpu_custom_call" | custom-call | tf_op jit(solution)/shard_map/factor/pallas_call | solution.py:312
  40.3 18.1 %coeffs.1 = bf16[512,256]{1,0:T(8,128)(2,1)S(1)} custom-call(bf16[512,256]{1,0:T(8,128)(2,1)S(1)} %get-tuple-element.14.partial), custom_call_target="tpu_custom_call" | custom-call | tf_op jit(solution)/shard_map/coeffs/pallas_call | solution.py:331
  58.4 1.0 %copy.7 = f32[1,256,512]{2,1,0:T(8,128)} copy(f32[1,256,512]{1,2,0:T(8,128)S(1)} %convert_bitcast_fusion) | data formatting | bytes 1048576
  (1 shorter events, 0.0 us)
Async XLA Ops:
  0.6 0.7 %copy-start.2 = (f32[1,256]{1,0:T(1,128)S(1)}, f32[1,256]{1,0:T(1,128)}, u32[]{:S(2)}) copy-start(f32[1,256]{1,0:T(1,128)} %rates.1) | copy-start | bytes 3076
  0.6 0.7 %copy-start.3 = (s32[63]{0:T(128)S(1)}, s32[63]{0:T(128)}, u32[]{:S(2)}) copy-start(s32[63]{0:T(128)} %param.5) | copy-start | bytes 760
  1.3 1.0 %copy-start = (bf16[256,512]{1,0:T(8,128)(2,1)S(1)}, bf16[256,512]{1,0:T(8,128)(2,1)}, u32[]{:S(2)}) copy-start(bf16[256,512]{1,0:T(8,128)(2,1)} %frames.1) | copy-start | bytes 786436
  2.3 0.9 %copy-start.1 = (bf16[512,256]{1,0:T(8,128)(2,1)S(1)}, bf16[512,256]{1,0:T(8,128)(2,1)}, u32[]{:S(2)}) copy-start(bf16[512,256]{1,0:T(8,128)(2,1)} %sketch.3) | copy-start | bytes 786436
